TPU v7x, 32 devices: a whole 2x2x4 slice. The times are simulated.
32 devices in a mesh: groups: 2 (over x), fsdp: 16 (over z, y, core).
Axes of the slice: x: 2, y: 2, z: 4, core: 2. Of those that a mesh axis runs over, the one named last changes fastest.
Arguments:
- step_hidden: bfloat16 [16384, 4096], P(('groups', 'fsdp')), parts along dimension 0, may hold values from -6 to 6
- prm_cache: bfloat16 [512, 128, 1024], P(('groups', 'fsdp')), parts along dimension 0, may hold values from -256 to 256
- lengths: int32 [512], P(('groups', 'fsdp')), parts along dimension 0, may hold values from 32 to 128
- w_query: bfloat16 [4096, 2048], P('fsdp'), may hold values from -0.09375 to 0.09375
- w_keyval: bfloat16 [4096, 1024], P('fsdp'), may hold values from -0.09375 to 0.09375
- reward_head: float32 [2048], replicated, may hold values from -0.125 to 0.125
- placement: int32 [512], P('groups'), parts along dimension 0, may hold values from 0 to 255, each once
- parents: int32 [512], P('groups'), parts along dimension 0, may hold values from 0 to 255, as said below
- page_table: int32 [512, 2], P(('groups', 'fsdp')), parts along dimension 0, may hold values from 0 to 31, as said below
- policy_pool: bfloat16 [1024, 64, 1024], P(('groups', 'fsdp')), parts along dimension 0, may hold values from -6 to 6
- new_query: bfloat16 [512, 2, 2048], P(('groups', 'fsdp')), parts along dimension 0, may hold values from -180 to 180
- new_keyval: bfloat16 [512, 2, 1024], P(('groups', 'fsdp')), parts along dimension 0, may hold values from -6 to 6
Outputs:
- rewards: float32 [512], P(('groups', 'fsdp')), parts along dimension 0
- decoded: bfloat16 [512, 2, 2048], P(('groups', 'fsdp')), parts along dimension 0
There are 2 independent parts, one for each index of `groups`. A program takes and returns all parts, laid end to end along the dimension named above; an argument that names none is the same for every part. Nothing has to cross between parts.
Inputs may be any that keep to these rules, and one draw needn't show every extreme that they name: The rows that one device's slots name in page_table cover each of that device's 16 * 2 pool rows once. The 16 children d * 16 to d * 16 + 15 of one device have parent slots on distinct devices (parents[c] // 16); in every draw some device holds the parent of one child of every device.
All inputs are finite; a program needn't handle non-finite values.
Results may differ from a plain program's by a relative error of at most 0.012.
Values may be sent and summed in bfloat16 or wider, within the bound.
A program may use at most 192 MiB of HBM per device.

v0:
```python
import functools
import math

import jax
import jax.numpy as jnp
from jax import lax
from jax.experimental import pallas as pl
from jax.experimental.pallas import tpu as pltpu
from jax.sharding import PartitionSpec as P

HQ = 16
HD = 128
EPS = 1e-05
SCALE = 1.0 / math.sqrt(HD)
LOW = -1e30


def dot_last(a, b):
    return lax.dot_general(a, b, (((1,), (1,)), ((), ())), preferred_element_type=jnp.float32)


def spread_heads(rows, mask):
    tiled = jnp.concatenate([rows] * (mask.shape[1] // HD), axis=1)
    return jnp.where(mask, tiled, jnp.zeros_like(tiled))


def exchange_kernel(
    n,
    src_child,
    row_slot,
    lengths,
    pages,
    own_dev,
    rows_ref,
    wq_ref,
    query_ref,
    keyval_ref,
    pool_ref,
    decoded_ref,
    q_ref,
    qsend,
    qrecv,
    rrecv,
    wq2,
    psend,
    precv,
    osend,
    orecv,
    lsend,
    lrecv,
    send_sem,
    recv_sem,
    wq_sem,
):
    me = lax.axis_index("fsdp")
    core = lax.rem(me, 2)
    sibling = me + 1 - 2 * core
    pair = lax.div(me, 2)
    barrier = pltpu.get_barrier_semaphore()
    half = wq2.shape[2]
    beams = query_ref.shape[0]

    def greet(k, c):
        pl.semaphore_signal(barrier, inc=1, device_id={"fsdp": lax.rem(me + k, n)})
        return c

    lax.fori_loop(1, n, greet, 0)

    def fill(j, c):
        qsend[j] = query_ref[src_child[j]]
        return c

    lax.fori_loop(0, n, fill, 0)
    pl.semaphore_wait(barrier, n - 1)

    def copy(lane, k, src, dst, sender_view=True):
        peer = lax.rem(me + k, n)
        return pltpu.make_async_remote_copy(
            src_ref=src,
            dst_ref=dst,
            send_sem=send_sem.at[lane, k],
            recv_sem=recv_sem.at[lane, k],
            device_id={"fsdp": peer},
        )

    def peer_of(k):
        return lax.rem(me + k, n)

    def rows_copy(k):
        return copy(0, k, rows_ref.at[lax.div(peer_of(k), 2)], rrecv.at[me])

    def q_copy(k):
        return copy(1, k, qsend.at[peer_of(k)], qrecv.at[me])

    def p_copy(k):
        return copy(2, k, psend.at[peer_of(k)], precv.at[me])

    def o_copy(k):
        return copy(3, k, osend.at[peer_of(k)], orecv.at[me])

    def l_copy(k):
        return copy(4, k, lsend.at[peer_of(k)], lrecv.at[me])

    def start_all(*makers):
        def body(k, c):
            for maker in makers:
                maker(k).start()
            return c

        lax.fori_loop(1, n, body, 0)

    def wait_all(*makers):
        def body(k, c):
            for maker in makers:
                maker(k).wait()
            return c

        lax.fori_loop(1, n, body, 0)

    wq_copy = pltpu.make_async_remote_copy(
        src_ref=wq_ref.at[:, pl.ds(pl.multiple_of((1 - core) * half, half), half)],
        dst_ref=wq2.at[core],
        send_sem=wq_sem.at[0],
        recv_sem=wq_sem.at[1],
        device_id={"fsdp": sibling},
    )
    wq_copy.start()
    start_all(rows_copy)
    start_all(q_copy)
    wq2[core] = wq_ref[:, pl.ds(pl.multiple_of(core * half, half), half)]
    rrecv[me] = rows_ref[pair]
    qrecv[me] = qsend[me]

    square = jnp.zeros((rows_ref.shape[1], 1), jnp.float32)
    for k in range(n // 2):
        part = rows_ref[k].astype(jnp.float32)
        square = square + jnp.sum(part * part, axis=1, keepdims=True)
    row_scale = lax.rsqrt(square / (rows_ref.shape[2] * (n // 2)) + EPS)

    wq_copy.wait()
    wait_all(rows_copy)
    depth = wq_ref.shape[0]
    arrived_rows = rrecv[...].reshape(n * rrecv.shape[1], rrecv.shape[2])
    weights_pair = wq2[...].reshape(2 * depth, half)
    step_cols = min(512, half)
    for c0 in range(0, half, step_cols):
        part = jnp.dot(
            arrived_rows, weights_pair[:, c0 : c0 + step_cols], preferred_element_type=jnp.float32
        ).astype(jnp.bfloat16)
        psend[:, :, c0 : c0 + step_cols] = part.reshape(n, rrecv.shape[1], step_cols)
    start_all(p_copy)
    precv[me] = psend[me]

    count = query_ref.shape[1]
    kv_width = pool_ref.shape[2] // 2
    row_id = lax.broadcasted_iota(jnp.int32, (count, kv_width), 0)
    col_id = lax.broadcasted_iota(jnp.int32, (count, kv_width), 1)
    group = HQ // (kv_width // HD)
    head_mask = (row_id % HQ) // group == col_id // HD
    row_small = lax.broadcasted_iota(jnp.int32, (count, HD), 0)
    col_small = lax.broadcasted_iota(jnp.int32, (count, HD), 1)
    eye = row_small == col_small
    kv_row = (row_small % HQ) // group

    wait_all(q_copy)
    page_rows = pool_ref.shape[1]
    token = lax.broadcasted_iota(jnp.int32, (count, 2 * page_rows), 1)

    def attend(i):
        slot = row_slot[i]
        first = pages[2 * slot]
        second = pages[2 * slot + 1]
        keys = jnp.concatenate([pool_ref[first, :, :kv_width], pool_ref[second, :, :kv_width]], axis=0)
        values = jnp.concatenate([pool_ref[first, :, kv_width:], pool_ref[second, :, kv_width:]], axis=0)
        s = dot_last(spread_heads(qrecv[i], head_mask), keys) * SCALE
        usable = token < lengths[slot]
        s = jnp.where(usable, s, LOW)
        peak = jnp.max(s, axis=1, keepdims=True)
        w = jnp.where(usable, jnp.exp(s - peak), 0.0)
        total = jnp.sum(w, axis=1, keepdims=True)
        wide = jnp.dot(w.astype(jnp.bfloat16), values, preferred_element_type=jnp.float32)
        wide = jnp.where(head_mask, wide, 0.0)
        out = wide[:, :HD]
        for g in range(1, kv_width // HD):
            out = out + wide[:, g * HD : (g + 1) * HD]
        osend[i] = (out / total).astype(jnp.bfloat16)
        log_total = peak + jnp.log(total)
        log_row = jnp.sum(jnp.where(eye, log_total, 0.0), axis=0, keepdims=True)
        lsend[i] = jnp.broadcast_to(log_row, (8, HD))

    def attend_four(b, c):
        for u in range(4):
            attend(b * 4 + u)
        return c

    lax.fori_loop(0, n // 4, attend_four, 0)
    start_all(l_copy, o_copy)
    orecv[me] = osend[me]
    lrecv[me] = lsend[me]
    wait_all(l_copy, o_copy)

    def finish(c):
        dev = own_dev[c]
        remote = orecv[dev].astype(jnp.float32)
        log_col = jnp.sum(jnp.where(eye, lrecv[dev][0:1, :], 0.0), axis=1, keepdims=True)
        q = query_ref[c].astype(jnp.float32)
        kv = keyval_ref[c].astype(jnp.float32)

        def expand(base):
            full = jnp.zeros((count, HD), jnp.float32)
            for g in range(kv_width // HD):
                full = jnp.where(kv_row == g, kv[base + g : base + g + 1, :], full)
            return full

        kv_heads = kv_width // HD
        scores = []
        for j in range(count // HQ):
            s = jnp.sum(q * expand(2 * j * kv_heads), axis=1, keepdims=True) * SCALE
            scores.append(jnp.where(row_small[:, :1] >= j * HQ, s, LOW))
        top = log_col
        for s in scores:
            top = jnp.maximum(top, s)
        weight = jnp.exp(log_col - top)
        acc = weight * remote
        den = weight
        for j, s in enumerate(scores):
            p = jnp.where(row_small[:, :1] >= j * HQ, jnp.exp(s - top), 0.0)
            den = den + p
            acc = acc + p.astype(jnp.bfloat16).astype(jnp.float32) * expand((2 * j + 1) * kv_heads)
        decoded_ref[c] = (acc / den).astype(jnp.bfloat16)

    def finish_four(b, c):
        for u in range(4):
            finish(b * 4 + u)
        return c

    lax.fori_loop(0, beams // 4, finish_four, 0)

    wait_all(p_copy)
    for side in range(2):
        total = precv[side].astype(jnp.float32)
        for k in range(1, n // 2):
            total = total + precv[2 * k + side].astype(jnp.float32)
        q_ref[:, side * half : (side + 1) * half] = (total * row_scale).astype(jnp.bfloat16)


def reward_kernel(
    n,
    lengths,
    place,
    hidden_ref,
    weights_ref,
    cache_ref,
    q_ref,
    head_ref,
    out_ref,
    fresh,
    cached_score,
    cached_value,
    qbd_all,
    mine,
    every,
    send_sem,
    recv_sem,
):
    me = lax.axis_index("fsdp")
    barrier = pltpu.get_barrier_semaphore()

    def greet(k, c):
        pl.semaphore_signal(barrier, inc=1, device_id={"fsdp": lax.rem(me + k, n)})
        return c

    lax.fori_loop(1, n, greet, 0)
    beams, cache_len, width = cache_ref.shape
    kv_width = width // 2
    group = HQ // (kv_width // HD)
    row_id = lax.broadcasted_iota(jnp.int32, (HQ, kv_width), 0)
    col_id = lax.broadcasted_iota(jnp.int32, (HQ, kv_width), 1)
    head_mask = row_id // group == col_id // HD
    token = lax.broadcasted_iota(jnp.int32, (HQ, cache_len), 1)

    def beam(b):
        q16 = q_ref[b]
        qbd = spread_heads(q16, head_mask)
        qbd_all[b] = qbd
        s = dot_last(qbd, cache_ref[b, :, :kv_width]) * SCALE
        cached_score[b] = jnp.where(token < lengths[b], s, LOW)
        v = dot_last(head_ref[...], cache_ref[b, :, kv_width:])
        cached_value[b] = v[:HQ] + v[HQ:]

    def beam_four(i, c):
        for u in range(4):
            beam(i * 4 + u)
        return c

    lax.fori_loop(0, beams // 4, beam_four, 0)

    row_count = hidden_ref.shape[0]
    block = row_count // 2

    def project(i, c):
        at = pl.ds(pl.multiple_of(i * block, block), block)
        x = hidden_ref[at, :]
        wide = x.astype(jnp.float32)
        scale = lax.rsqrt(jnp.mean(wide * wide, axis=1, keepdims=True) + EPS)
        fresh[at, :] = jnp.dot(x, weights_ref[...], preferred_element_type=jnp.float32) * scale
        return c

    lax.fori_loop(0, 2, project, 0)

    total_rows = beams * HQ
    step_len = row_count // beams
    fresh_keys = fresh[:, :kv_width].astype(jnp.bfloat16)
    sf = dot_last(qbd_all[...].reshape(total_rows, kv_width), fresh_keys) * SCALE
    r = lax.broadcasted_iota(jnp.int32, (total_rows, row_count), 0)
    k = lax.broadcasted_iota(jnp.int32, (total_rows, row_count), 1)
    same = r // HQ == k // step_len
    sf = jnp.where(same, sf, LOW)
    sc = cached_score[...].reshape(total_rows, cache_len)
    peak = jnp.maximum(jnp.max(sf, axis=1, keepdims=True), jnp.max(sc, axis=1, keepdims=True))
    wf = jnp.where(same, jnp.exp(sf - peak), 0.0)
    wc = jnp.where(sc > 0.5 * LOW, jnp.exp(sc - peak), 0.0)
    vt = jnp.transpose(fresh[:, kv_width : kv_width + HD])
    vf = vt[:HQ] + vt[HQ : 2 * HQ]
    vf = jnp.broadcast_to(vf[None], (beams, HQ, row_count)).reshape(total_rows, row_count)
    vc = cached_value[...].reshape(total_rows, cache_len)
    den = jnp.sum(wf, axis=1, keepdims=True) + jnp.sum(wc, axis=1, keepdims=True)
    num = jnp.sum(wf * vf, axis=1, keepdims=True) + jnp.sum(wc * vc, axis=1, keepdims=True)
    ratio = num / den
    rr = lax.broadcasted_iota(jnp.int32, (total_rows, HD), 0)
    cc = lax.broadcasted_iota(jnp.int32, (total_rows, HD), 1)
    row = jnp.sum(jnp.where(rr // HQ == cc, ratio, 0.0), axis=0, keepdims=True)
    mine[...] = jnp.broadcast_to(row, (8, HD))
    every[me] = mine[...]

    pl.semaphore_wait(barrier, n - 1)

    def copy(k):
        return pltpu.make_async_remote_copy(
            src_ref=mine,
            dst_ref=every.at[me],
            send_sem=send_sem.at[k],
            recv_sem=recv_sem.at[k],
            device_id={"fsdp": lax.rem(me + k, n)},
        )

    def start(k, c):
        copy(k).start()
        return c

    def wait(k, c):
        copy(k).wait()
        return c

    lax.fori_loop(1, n, start, 0)
    lax.fori_loop(1, n, wait, 0)
    lane = lax.broadcasted_iota(jnp.int32, (1, HD), 1)
    for b in range(beams):
        spot = place[b]
        got = every[lax.div(spot, beams)][0:1, :]
        out_ref[b : b + 1, :] = jnp.broadcast_to(
            jnp.sum(jnp.where(lane == lax.rem(spot, beams), got, 0.0), axis=1, keepdims=True), (1, HD)
        )


def split_two(x):
    high = x.astype(jnp.bfloat16)
    return high, (x - high.astype(jnp.float32)).astype(jnp.bfloat16)


def shards(
    step_hidden,
    prm_cache,
    lengths,
    w_query,
    w_keyval,
    reward_head,
    placement,
    parents,
    page_table,
    policy_pool,
    new_query,
    new_keyval,
):
    me = lax.axis_index("fsdp")
    n = lax.axis_size("fsdp")
    beams = lengths.shape[0]
    step_len = step_hidden.shape[0] // beams
    width = step_hidden.shape[1]
    kv_width = w_keyval.shape[1] // 2
    kv_heads = kv_width // HD
    group = HQ // kv_heads
    depth = w_query.shape[0]
    half = w_query.shape[1] // 2
    new = new_query.shape[1]
    bf16, f32 = jnp.bfloat16, jnp.float32

    head_rows = reward_head.reshape(HQ, HD)
    head_mask = (jnp.arange(HQ)[:, None] // group) == (jnp.arange(kv_width)[None, :] // HD)
    head_wide = jnp.where(head_mask, jnp.tile(head_rows, (1, kv_heads)), 0.0)
    head_two = jnp.concatenate(split_two(head_wide), axis=0)
    folded = dot_last(w_keyval[:, kv_width:], head_two)
    folded = folded[:, :HQ] + folded[:, HQ:]
    pieces = split_two(folded)
    own_weights = jnp.concatenate(
        [w_keyval[:, :kv_width], pieces[0], pieces[1], jnp.zeros((depth, HD - 2 * HQ), bf16)], axis=1
    )
    weights = lax.all_gather(own_weights, "fsdp", axis=0, tiled=True)

    last = step_hidden.reshape(beams, step_len, width)[:, step_len - 1]
    rows = last.reshape(beams, n // 2, 2 * depth).transpose(1, 0, 2)
    parent_dev = parents // beams
    parent_inner = parents % beams
    serves = parent_dev.reshape(n, beams) == me
    row_slot = jnp.sum(jnp.where(serves, parent_inner.reshape(n, beams), 0), axis=1)
    own_dev = lax.dynamic_slice_in_dim(parent_dev, me * beams, beams)
    chosen = jnp.arange(n, dtype=jnp.int32)[:, None] == own_dev[None, :]
    src_child = jnp.sum(jnp.where(chosen, jnp.arange(beams, dtype=jnp.int32)[None, :], 0), axis=1)

    smem = pl.BlockSpec(memory_space=pltpu.SMEM)
    vmem = pl.BlockSpec(memory_space=pltpu.VMEM)
    count = new * HQ
    decoded, q = pl.pallas_call(
        functools.partial(exchange_kernel, n),
        out_shape=(
            jax.ShapeDtypeStruct((beams, count, HD), bf16),
            jax.ShapeDtypeStruct((beams, 2 * half), bf16),
        ),
        in_specs=[smem] * 5 + [vmem] * 5,
        out_specs=(vmem, vmem),
        scratch_shapes=[
            pltpu.VMEM((n, count, HD), bf16),
            pltpu.VMEM((n, count, HD), bf16),
            pltpu.VMEM((n, beams, 2 * depth), bf16),
            pltpu.VMEM((2, depth, half), bf16),
            pltpu.VMEM((n, beams, half), bf16),
            pltpu.VMEM((n, beams, half), bf16),
            pltpu.VMEM((n, count, HD), bf16),
            pltpu.VMEM((n, count, HD), bf16),
            pltpu.VMEM((n, 8, HD), f32),
            pltpu.VMEM((n, 8, HD), f32),
            pltpu.SemaphoreType.DMA((5, n)),
            pltpu.SemaphoreType.DMA((5, n)),
            pltpu.SemaphoreType.DMA((2,)),
        ],
        compiler_params=pltpu.CompilerParams(
            collective_id=0, has_side_effects=True, vmem_limit_bytes=28 * 2**20
        ),
        cost_estimate=pl.CostEstimate(flops=10**9, bytes_accessed=8 * 2**20, transcendentals=0),
    )(
        src_child,
        row_slot,
        lengths,
        page_table.reshape(-1),
        own_dev,
        rows,
        w_query,
        new_query.reshape(beams, count, HD),
        new_keyval.reshape(beams, new * 2 * kv_heads, HD),
        policy_pool,
    )

    my_place = lax.dynamic_slice_in_dim(placement, me * beams, beams)
    cache_len = prm_cache.shape[1]
    rewards = pl.pallas_call(
        functools.partial(reward_kernel, n),
        out_shape=jax.ShapeDtypeStruct((beams, HD), f32),
        in_specs=[smem] * 2 + [vmem] * 5,
        out_specs=vmem,
        scratch_shapes=[
            pltpu.VMEM((beams * step_len, kv_width + HD), f32),
            pltpu.VMEM((beams, HQ, cache_len), f32),
            pltpu.VMEM((beams, HQ, cache_len), f32),
            pltpu.VMEM((beams, HQ, kv_width), bf16),
            pltpu.VMEM((8, HD), f32),
            pltpu.VMEM((n, 8, HD), f32),
            pltpu.SemaphoreType.DMA((n,)),
            pltpu.SemaphoreType.DMA((n,)),
        ],
        compiler_params=pltpu.CompilerParams(
            collective_id=1, has_side_effects=True, vmem_limit_bytes=36 * 2**20
        ),
        cost_estimate=pl.CostEstimate(flops=3 * 10**9, bytes_accessed=14 * 2**20, transcendentals=0),
    )(lengths, my_place, step_hidden, weights, prm_cache, q.reshape(beams, HQ, HD), head_two)
    return (rewards[:, 0], decoded.reshape(beams, new, HQ * HD))


def solution(mesh):
    in_specs = (
        P(("groups", "fsdp"), None),
        P(("groups", "fsdp"), None, None),
        P(("groups", "fsdp")),
        P("fsdp", None),
        P("fsdp", None),
        P(),
        P("groups"),
        P("groups"),
        P(("groups", "fsdp"), None),
        P(("groups", "fsdp"), None, None),
        P(("groups", "fsdp"), None, None),
        P(("groups", "fsdp"), None, None),
    )
    out_specs = (P(("groups", "fsdp")), P(("groups", "fsdp"), None, None))
    return jax.shard_map(shards, mesh=mesh, in_specs=in_specs, out_specs=out_specs, check_vma=False)
```

profile of v0, /device:TPU:0, one launch (start us, length us, event | category | flops | bytes accessed | tf_op | source)
XLA Modules:
  0.0 109.2 jit_solution(6970822311583347214)
XLA Ops:
  7.2 0.0 copy-start.4
  7.2 0.0 all-gather.2.cloned.1.call-start
  7.2 0.8 tile.11
  8.0 0.1 subtract_convert_fusion.1
  8.1 0.1 fusion.1
  8.2 1.0 slice.18
  9.1 1.1 %convolution_bitcast_fusion = f32[256,32]{0,1:T(8,128)S(1)} fusion(bf16[256,1024]{1,0:T(8,128)(2,1)} %param.16, bf16[16,512]{1,0:T(8,128)(2,1)S(1)} %subtract_convert_fusion.1, bf16[16,512]{1,0:T(8,128)(2,1)S(1)} %fusion.1), kind=kOutput, calls=%fused_computation | convolution fusion | flops 8454144 | bytes 327680 | tf_op jit(solution)/shard_map/dot_general | solution.py:19
  10.3 0.1 copy.24
  10.4 0.0 copy-start.6
  10.4 0.1 pad.3.clone
  10.5 0.8 maximum_maximum_fusion
  11.3 0.0 all-gather.2.cloned.1.call-update
  11.4 0.8 dynamic_slice.6.place
  12.1 0.7 compare_select_fusion
  12.8 0.1 dynamic_slice.7.own_dev
  12.9 0.1 select_n.59
  13.0 0.1 reduce_sum.19.row_slot
  13.1 0.8 copy.26
  13.8 0.1 reshape.107.pages
  13.9 0.9 reshape.110.keyval_ref
  14.8 1.0 reshape.109.query_ref
  15.8 2.0 %slice_reduce_fusion = bf16[16,4096]{1,0:T(8,128)(2,1)S(1)} fusion(bf16[16,32,4096]{2,1,0:T(8,128)(2,1)} %bitcast.22), kind=kLoop, calls=%fused_computation.2 | loop fusion | bytes 262144 | tf_op jit(solution)/shard_map/slice | solution.py:410
  17.9 0.1 select_reduce_fusion.src_child
  18.0 0.0 copy-done.4
  18.0 0.0 copy-start.3
  18.0 2.2 %copy-done.3 = bf16[32,64,1024]{2,1,0:T(8,128)(2,1)S(1)} copy-done((bf16[32,64,1024]{2,1,0:T(8,128)(2,1)S(1)}, bf16[32,64,1024]{2,1,0:T(8,128)(2,1)}, u32[]{:S(2)}) %copy-start.3) | copy-done | bytes 4194328
  20.2 0.0 copy-start.5
  20.2 0.7 copy-done.5
  20.8 47.5 %shard_map.131 = (bf16[16,32,128]{2,1,0:T(8,128)(2,1)S(1)}, bf16[16,2048]{1,0:T(8,128)(2,1)S(1)}) custom-call(s32[16]{0:T(128)S(1)} %select_reduce_fusion.src_child, s32[16]{0:T(128)S(1)} %reduce_sum.19.row_slot, s32[16]{0:T(128)S(1)} %copy-done.5, s32[32]{0:T(128)S(1)} %reshape.107.pages, s32[16]{0:T(128)S(1)} %dynamic_slice.7.own_dev, ...), custom_call_target="tpu_custom_call" | custom-call | flops 1000000000 | bytes 8388608 | tf_op jit(solution)/shard_map/pallas_call | solution.py:423
  68.4 0.7 reshape.112
  69.1 14.4 %all-gather.2.cloned.1.call-done.weights_ref = bf16[4096,640]{1,0:T(8,128)(2,1)} async-done(((bf16[256,640]{1,0:T(8,128)(2,1)}), bf16[4096,640]{1,0:T(8,128)(2,1)}) %all-gather.2.cloned.1.call-update) | async-done | bytes 5242896 | tf_op jit(solution)/shard_map/all_gather | solution.py:408
  83.5 0.0 copy-done.6
  83.5 0.0 copy-start
  83.5 2.5 %copy-done = bf16[4096,640]{1,0:T(8,128)(2,1)S(1)} copy-done((bf16[4096,640]{1,0:T(8,128)(2,1)S(1)}, bf16[4096,640]{1,0:T(8,128)(2,1)}, u32[]{:S(2)}) %copy-start) | copy-done | bytes 5242904
  86.0 0.0 copy-start.1
  86.0 2.2 %copy-done.1 = bf16[512,4096]{1,0:T(8,128)(2,1)S(1)} copy-done((bf16[512,4096]{1,0:T(8,128)(2,1)S(1)}, bf16[512,4096]{1,0:T(8,128)(2,1)}, u32[]{:S(2)}) %copy-start.1) | copy-done | bytes 4194328
  88.2 0.0 copy-start.2
  88.2 2.2 %copy-done.2 = bf16[16,128,1024]{2,1,0:T(8,128)(2,1)S(1)} copy-done((bf16[16,128,1024]{2,1,0:T(8,128)(2,1)S(1)}, bf16[16,128,1024]{2,1,0:T(8,128)(2,1)}, u32[]{:S(2)}) %copy-start.2) | copy-done | bytes 4194328
  90.4 11.3 %shard_map.132 = f32[16,128]{1,0:T(8,128)S(1)} custom-call(s32[16]{0:T(128)S(1)} %copy-done.6, s32[16]{0:T(128)S(1)} %dynamic_slice.6.place, bf16[512,4096]{1,0:T(8,128)(2,1)S(1)} %copy-done.1, bf16[4096,640]{1,0:T(8,128)(2,1)S(1)} %copy-done, bf16[16,128,1024]{2,1,0:T(8,128)(2,1)S(1)} %copy-done.2, bf16[16,16,128]{2,1,0:T(8,128)(2,1)S(1)} %bitcast.24, ...), custom_call_target="tpu_custom_call" | custom-call | flops 3000000000 | bytes 14680064 | tf_op jit(solution)/shard_map/pallas_call | solution.py:465
  101.7 0.6 slice_reduce_fusion.1
  (8 shorter events, 0.1 us)
Async XLA Ops:
  7.2 10.8 %copy-start.4 = (bf16[256,2048]{1,0:T(8,128)(2,1)S(1)}, bf16[256,2048]{1,0:T(8,128)(2,1)}, u32[]{:S(2)}) copy-start(bf16[256,2048]{1,0:T(8,128)(2,1)} %wq_ref.1) | copy-start | bytes 3145732
  7.2 76.3 %all-gather.2.cloned.1.call-start = ((), (), s32[]{:S(2)}) async-start(), calls=%async_computation | async-start | bytes 5570560 | tf_op jit(solution)/shard_map/all_gather | solution.py:408
  10.4 73.1 %copy-start.6 = (s32[16]{0:T(128)S(1)}, s32[16]{0:T(128)}, u32[]{:S(2)}) copy-start(s32[16]{0:T(128)} %lengths.3) | copy-start | bytes 196
  18.0 2.2 %copy-start.3 = (bf16[32,64,1024]{2,1,0:T(8,128)(2,1)S(1)}, bf16[32,64,1024]{2,1,0:T(8,128)(2,1)}, u32[]{:S(2)}) copy-start(bf16[32,64,1024]{2,1,0:T(8,128)(2,1)} %pool_ref.1) | copy-start | bytes 12582916
  20.2 0.7 copy-start.5
  83.5 2.5 %copy-start = (bf16[4096,640]{1,0:T(8,128)(2,1)S(1)}, bf16[4096,640]{1,0:T(8,128)(2,1)}, u32[]{:S(2)}) copy-start(bf16[4096,640]{1,0:T(8,128)(2,1)} %all-gather.2.cloned.1.call-done.weights_ref) | copy-start | bytes 15728644
  86.0 2.2 %copy-start.1 = (bf16[512,4096]{1,0:T(8,128)(2,1)S(1)}, bf16[512,4096]{1,0:T(8,128)(2,1)}, u32[]{:S(2)}) copy-start(bf16[512,4096]{1,0:T(8,128)(2,1)} %hidden_ref.1) | copy-start | bytes 12582916
  88.2 2.2 %copy-start.2 = (bf16[16,128,1024]{2,1,0:T(8,128)(2,1)S(1)}, bf16[16,128,1024]{2,1,0:T(8,128)(2,1)}, u32[]{:S(2)}) copy-start(bf16[16,128,1024]{2,1,0:T(8,128)(2,1)} %cache_ref.1) | copy-start | bytes 12582916
Sparse Core Ops, SparseCore 0:
  11.5 71.9 all-gather.1
where the time goes:
time: 110 us; the launch traced here: 109 us
  Pallas kernels  58.8 us (53%)
  local copies, waits for them, and re-layouts  18.6 us (17%)
  waiting for transfers between devices  14.4 us (13%)
  between operations  14.2 us (13%)
  other arithmetic  1.93 us (2%)
  matrix products  1.12 us (1%)
    pallas_call x1, Pallas kernels, shards(): pl.pallas_call(functools.partial(exchange_kernel, n), out_shape=(jax.Shap...  47.5 us
    all_gather x1, waiting for transfers between devices, shards(): weights = lax.all_gather(own_weights, 'fsdp', axis=0, tiled=True)  14.4 us
    pallas_call x1, Pallas kernels, shards(): pl.pallas_call(functools.partial(reward_kernel, n), out_shape=jax.ShapeDt...  11.3 us
    unnamed x16, local copies, waits for them, and re-layouts  10.5 us
  transfers between devices with their start and end apart: 1, of which 1 were waited for; matrix products, arithmetic and copies ran while one was open for 7% of the time, Pallas kernels for 43%

commit v1 on v0

v1 whole, which is shorter than its diff:
```python
import functools
import math

import jax
import jax.numpy as jnp
from jax import lax
from jax.experimental import pallas as pl
from jax.experimental.pallas import tpu as pltpu
from jax.sharding import PartitionSpec as P

HQ = 16
HD = 128
EPS = 1e-05
SCALE = 1.0 / math.sqrt(HD)
LOW = -1e30


def dot_last(a, b):
    return lax.dot_general(a, b, (((1,), (1,)), ((), ())), preferred_element_type=jnp.float32)


def spread_heads(rows, mask):
    tiled = jnp.concatenate([rows] * (mask.shape[1] // HD), axis=1)
    return jnp.where(mask, tiled, jnp.zeros_like(tiled))


def score_kernel(
    n,
    lengths,
    pages,
    place,
    parents,
    rows_ref,
    wq_ref,
    wkv_ref,
    head_ref,
    query_ref,
    keyval_ref,
    hidden_hbm,
    cache_hbm,
    pool_hbm,
    decoded_ref,
    out_ref,
    hidden_ref,
    cache_ref,
    pool_ref,
    weights,
    fresh,
    cached_score,
    cached_value,
    qbd_all,
    q_heads,
    mine,
    every,
    qsend,
    qrecv,
    rrecv,
    wq2,
    psend,
    precv,
    osend,
    orecv,
    lsend,
    lrecv,
    send_sem,
    recv_sem,
    wq_sem,
    z_sem,
    y_sem,
    c_sem,
    load_sem,
):
    me = lax.axis_index("fsdp")
    core = lax.rem(me, 2)
    sibling = me + 1 - 2 * core
    pair = lax.div(me, 2)
    across = me + 2 - 4 * lax.rem(pair, 2)
    low = lax.rem(me, 4)
    column = lax.div(me, 4)
    columns = n // 4
    barrier = pltpu.get_barrier_semaphore()
    half = wq2.shape[2]
    beams = query_ref.shape[0]
    depth = wq_ref.shape[0]

    def greet(k, c):
        pl.semaphore_signal(barrier, inc=1, device_id={"fsdp": lax.rem(me + k, n)})
        return c

    lax.fori_loop(1, n, greet, 0)

    loads = [
        pltpu.make_async_copy(src, dst, load_sem.at[i])
        for i, (src, dst) in enumerate(
            [(pool_hbm, pool_ref), (cache_hbm, cache_ref), (hidden_hbm, hidden_ref)]
        )
    ]
    for load in loads:
        load.start()

    def fill(j, c):
        pick = jnp.int32(0)
        for child in range(beams):
            hit = lax.div(parents[me * beams + child], beams) == j
            pick = jnp.maximum(pick, jnp.where(hit, child, 0))
        qsend[j] = query_ref[pick]
        return c

    lax.fori_loop(0, n, fill, 0)

    def peer_of(k):
        return lax.rem(me + k, n)

    def copy(lane, k, src, dst):
        return pltpu.make_async_remote_copy(
            src_ref=src,
            dst_ref=dst,
            send_sem=send_sem.at[lane, k],
            recv_sem=recv_sem.at[lane, k],
            device_id={"fsdp": peer_of(k)},
        )

    def rows_copy(k):
        return copy(0, k, rows_ref.at[lax.div(peer_of(k), 2)], rrecv.at[me])

    def q_copy(k):
        return copy(1, k, qsend.at[peer_of(k)], qrecv.at[me])

    def p_copy(k):
        return copy(2, k, psend.at[peer_of(k)], precv.at[me])

    def o_copy(k):
        return copy(3, k, osend.at[peer_of(k)], orecv.at[me])

    def l_copy(k):
        return copy(4, k, lsend.at[peer_of(k)], lrecv.at[me])

    def reward_copy(k):
        return copy(5, k, mine, every.at[me])

    def start_all(*makers):
        def body(k, c):
            for maker in makers:
                maker(k).start()
            return c

        lax.fori_loop(1, n, body, 0)

    def wait_all(*makers):
        def body(k, c):
            for maker in makers:
                maker(k).wait()
            return c

        lax.fori_loop(1, n, body, 0)

    def block_of(k, member):
        return lax.rem(column + columns - k, columns) * 4 + member

    def z_copy(k):
        return pltpu.make_async_remote_copy(
            src_ref=weights.at[me],
            dst_ref=weights.at[me],
            send_sem=z_sem.at[0, k],
            recv_sem=z_sem.at[1, k],
            device_id={"fsdp": lax.rem(column + k, columns) * 4 + low},
        )

    def y_copy(k):
        block = block_of(k, low)
        return pltpu.make_async_remote_copy(
            src_ref=weights.at[block],
            dst_ref=weights.at[block],
            send_sem=y_sem.at[0, k],
            recv_sem=y_sem.at[1, k],
            device_id={"fsdp": across},
        )

    def c_copy(side, k):
        block = block_of(k, low if side == 0 else lax.rem(low + 2, 4))
        return pltpu.make_async_remote_copy(
            src_ref=weights.at[block],
            dst_ref=weights.at[block],
            send_sem=c_sem.at[0, side, k],
            recv_sem=c_sem.at[1, side, k],
            device_id={"fsdp": sibling},
        )

    wq_copy = pltpu.make_async_remote_copy(
        src_ref=wq_ref.at[:, pl.ds(pl.multiple_of((1 - core) * half, half), half)],
        dst_ref=wq2.at[core],
        send_sem=wq_sem.at[0],
        recv_sem=wq_sem.at[1],
        device_id={"fsdp": sibling},
    )
    pl.semaphore_wait(barrier, n - 1)
    wq_copy.start()
    start_all(rows_copy)
    start_all(q_copy)

    beam_count, cache_len, width = cache_ref.shape
    kv_width = width // 2
    kv_heads = kv_width // HD
    group = HQ // kv_heads
    folded = dot_last(wkv_ref[:, kv_width:], head_ref[...])
    folded = folded + pltpu.roll(folded, HD - HQ, 1)
    high = folded.astype(jnp.bfloat16).astype(jnp.float32)
    lane_w = lax.broadcasted_iota(jnp.int32, (depth, HD), 1)
    rest = pltpu.roll(folded - high, HQ, 1)
    both = jnp.where(lane_w < HQ, high, jnp.where(lane_w < 2 * HQ, rest, 0.0))
    weights[me, :, :kv_width] = wkv_ref[:, :kv_width]
    weights[me, :, kv_width:] = both.astype(jnp.bfloat16)

    def z_start(k, c):
        z_copy(k).start()
        return c

    lax.fori_loop(1, columns, z_start, 0)
    y_copy(0).start()
    c_copy(0, 0).start()

    wq2[core] = wq_ref[:, pl.ds(pl.multiple_of(core * half, half), half)]
    rrecv[me] = rows_ref[pair]
    qrecv[me] = qsend[me]
    square = jnp.zeros((rows_ref.shape[1], 1), jnp.float32)
    for k in range(n // 2):
        part = rows_ref[k].astype(jnp.float32)
        square = square + jnp.sum(part * part, axis=1, keepdims=True)
    row_scale = lax.rsqrt(square / (rows_ref.shape[2] * (n // 2)) + EPS)

    wq_copy.wait()
    wait_all(rows_copy)
    arrived_rows = rrecv[...].reshape(n * rrecv.shape[1], rrecv.shape[2])
    weights_pair = wq2[...].reshape(2 * depth, half)
    step_cols = min(512, half)
    for c0 in range(0, half, step_cols):
        part = jnp.dot(
            arrived_rows, weights_pair[:, c0 : c0 + step_cols], preferred_element_type=jnp.float32
        ).astype(jnp.bfloat16)
        psend[:, :, c0 : c0 + step_cols] = part.reshape(n, rrecv.shape[1], step_cols)
    start_all(p_copy)
    precv[me] = psend[me]

    count = query_ref.shape[1]
    row_id = lax.broadcasted_iota(jnp.int32, (count, kv_width), 0)
    col_id = lax.broadcasted_iota(jnp.int32, (count, kv_width), 1)
    head_mask = (row_id % HQ) // group == col_id // HD
    row_small = lax.broadcasted_iota(jnp.int32, (count, HD), 0)
    col_small = lax.broadcasted_iota(jnp.int32, (count, HD), 1)
    eye = row_small == col_small
    kv_row = (row_small % HQ) // group

    loads[0].wait()
    wait_all(q_copy)
    page_rows = pool_ref.shape[1]
    token = lax.broadcasted_iota(jnp.int32, (count, 2 * page_rows), 1)

    def attend(i):
        slot = jnp.int32(0)
        for child in range(beams):
            parent = parents[i * beams + child]
            inner = lax.rem(parent, beams)
            slot = jnp.maximum(slot, jnp.where(lax.div(parent, beams) == me, inner, 0))
        first = pages[slot, 0]
        second = pages[slot, 1]
        keys = jnp.concatenate([pool_ref[first, :, :kv_width], pool_ref[second, :, :kv_width]], axis=0)
        values = jnp.concatenate([pool_ref[first, :, kv_width:], pool_ref[second, :, kv_width:]], axis=0)
        s = dot_last(spread_heads(qrecv[i], head_mask), keys) * SCALE
        usable = token < lengths[slot]
        s = jnp.where(usable, s, LOW)
        peak = jnp.max(s, axis=1, keepdims=True)
        w = jnp.where(usable, jnp.exp(s - peak), 0.0)
        total = jnp.sum(w, axis=1, keepdims=True)
        wide = jnp.dot(w.astype(jnp.bfloat16), values, preferred_element_type=jnp.float32)
        wide = jnp.where(head_mask, wide, 0.0)
        out = wide[:, :HD]
        for g in range(1, kv_heads):
            out = out + wide[:, g * HD : (g + 1) * HD]
        osend[i] = (out / total).astype(jnp.bfloat16)
        log_total = peak + jnp.log(total)
        log_row = jnp.sum(jnp.where(eye, log_total, 0.0), axis=0, keepdims=True)
        lsend[i] = jnp.broadcast_to(log_row, (8, HD))

    def attend_four(b, c):
        for u in range(4):
            attend(b * 4 + u)
        return c

    lax.fori_loop(0, n // 4, attend_four, 0)
    start_all(l_copy, o_copy)
    orecv[me] = osend[me]
    lrecv[me] = lsend[me]

    def z_pass(k, c):
        z_copy(k).wait()
        y_copy(k).start()
        c_copy(0, k).start()
        return c

    lax.fori_loop(1, columns, z_pass, 0)

    loads[1].wait()

    def cache_value(b, c):
        for u in range(4):
            v = dot_last(head_ref[: 2 * HQ, :], cache_ref[b * 4 + u, :, kv_width:])
            cached_value[b * 4 + u] = v[:HQ] + v[HQ : 2 * HQ]
        return c

    lax.fori_loop(0, beam_count // 4, cache_value, 0)
    wait_all(l_copy, o_copy)

    def finish(c):
        dev = lax.div(parents[me * beams + c], beams)
        remote = orecv[dev].astype(jnp.float32)
        log_col = jnp.sum(jnp.where(eye, lrecv[dev][0:1, :], 0.0), axis=1, keepdims=True)
        q = query_ref[c].astype(jnp.float32)
        kv = keyval_ref[c].astype(jnp.float32)

        def expand(base):
            full = jnp.zeros((count, HD), jnp.float32)
            for g in range(kv_heads):
                full = jnp.where(kv_row == g, kv[base + g : base + g + 1, :], full)
            return full

        scores = []
        for j in range(count // HQ):
            s = jnp.sum(q * expand(2 * j * kv_heads), axis=1, keepdims=True) * SCALE
            scores.append(jnp.where(row_small[:, :1] >= j * HQ, s, LOW))
        top = log_col
        for s in scores:
            top = jnp.maximum(top, s)
        weight = jnp.exp(log_col - top)
        acc = weight * remote
        den = weight
        for j, s in enumerate(scores):
            p = jnp.where(row_small[:, :1] >= j * HQ, jnp.exp(s - top), 0.0)
            den = den + p
            acc = acc + p.astype(jnp.bfloat16).astype(jnp.float32) * expand((2 * j + 1) * kv_heads)
        decoded_ref[c] = (acc / den).astype(jnp.bfloat16)

    def finish_four(b, c):
        for u in range(4):
            finish(b * 4 + u)
        return c

    lax.fori_loop(0, beams // 4, finish_four, 0)

    def y_pass(k, c):
        y_copy(k).wait()
        c_copy(1, k).start()
        return c

    lax.fori_loop(0, columns, y_pass, 0)

    wait_all(p_copy)
    for side in range(2):
        total = precv[side].astype(jnp.float32)
        for k in range(1, n // 2):
            total = total + precv[2 * k + side].astype(jnp.float32)
        total = (total * row_scale).astype(jnp.bfloat16).astype(jnp.float32)
        for h in range(half // HD):
            q_heads[:, side * (half // HD) + h, :] = total[:, h * HD : (h + 1) * HD]

    mask16 = head_mask[:HQ]
    token16 = lax.broadcasted_iota(jnp.int32, (HQ, cache_len), 1)

    def cache_scores(i, c):
        for u in range(4):
            b = i * 4 + u
            qbd = spread_heads(q_heads[b].astype(jnp.bfloat16), mask16)
            qbd_all[b] = qbd
            s = dot_last(qbd, cache_ref[b, :, :kv_width]) * SCALE
            cached_score[b] = jnp.where(token16 < lengths[b], s, LOW)
        return c

    lax.fori_loop(0, beam_count // 4, cache_scores, 0)

    loads[2].wait()

    def c_pass(k, c):
        c_copy(0, k).wait()
        c_copy(1, k).wait()
        return c

    lax.fori_loop(0, columns, c_pass, 0)

    row_count = hidden_ref.shape[0]
    block = row_count // 2
    depth_all = n * depth

    def project(i, c):
        at = pl.ds(pl.multiple_of(i * block, block), block)
        x = hidden_ref[at, :]
        wide = x.astype(jnp.float32)
        scale = lax.rsqrt(jnp.mean(wide * wide, axis=1, keepdims=True) + EPS)
        w_all = weights[...].reshape(depth_all, weights.shape[2])
        fresh[at, :] = jnp.dot(x, w_all, preferred_element_type=jnp.float32) * scale
        return c

    lax.fori_loop(0, 2, project, 0)

    total_rows = beams * HQ
    step_len = row_count // beams
    fresh_keys = fresh[:, :kv_width].astype(jnp.bfloat16)
    sf = dot_last(qbd_all[...].reshape(total_rows, kv_width), fresh_keys) * SCALE
    r = lax.broadcasted_iota(jnp.int32, (total_rows, row_count), 0)
    k = lax.broadcasted_iota(jnp.int32, (total_rows, row_count), 1)
    same = r // HQ == k // step_len
    sf = jnp.where(same, sf, LOW)
    sc = cached_score[...].reshape(total_rows, cache_len)
    peak = jnp.maximum(jnp.max(sf, axis=1, keepdims=True), jnp.max(sc, axis=1, keepdims=True))
    wf = jnp.where(same, jnp.exp(sf - peak), 0.0)
    wc = jnp.where(sc > 0.5 * LOW, jnp.exp(sc - peak), 0.0)
    vt = jnp.transpose(fresh[:, kv_width : kv_width + HD])
    vf = vt[:HQ] + vt[HQ : 2 * HQ]
    vf = jnp.broadcast_to(vf[None], (beams, HQ, row_count)).reshape(total_rows, row_count)
    vc = cached_value[...].reshape(total_rows, cache_len)
    den = jnp.sum(wf, axis=1, keepdims=True) + jnp.sum(wc, axis=1, keepdims=True)
    num = jnp.sum(wf * vf, axis=1, keepdims=True) + jnp.sum(wc * vc, axis=1, keepdims=True)
    ratio = num / den
    rr = lax.broadcasted_iota(jnp.int32, (total_rows, HD), 0)
    cc = lax.broadcasted_iota(jnp.int32, (total_rows, HD), 1)
    row = jnp.sum(jnp.where(rr // HQ == cc, ratio, 0.0), axis=0, keepdims=True)
    mine[...] = jnp.broadcast_to(row, (8, HD))
    every[me] = mine[...]
    start_all(reward_copy)
    wait_all(reward_copy)
    lane = lax.broadcasted_iota(jnp.int32, (1, HD), 1)
    for b in range(beams):
        spot = place[me * beams + b]
        got = every[lax.div(spot, beams)][0:1, :]
        out_ref[b : b + 1, :] = jnp.broadcast_to(
            jnp.sum(jnp.where(lane == lax.rem(spot, beams), got, 0.0), axis=1, keepdims=True), (1, HD)
        )


def split_two(x):
    high = x.astype(jnp.bfloat16)
    return high, (x - high.astype(jnp.float32)).astype(jnp.bfloat16)


def shards(
    step_hidden,
    prm_cache,
    lengths,
    w_query,
    w_keyval,
    reward_head,
    placement,
    parents,
    page_table,
    policy_pool,
    new_query,
    new_keyval,
):
    n = lax.axis_size("fsdp")
    beams, cache_len, _ = prm_cache.shape
    row_count, width = step_hidden.shape
    step_len = row_count // beams
    kv_width = w_keyval.shape[1] // 2
    kv_heads = kv_width // HD
    group = HQ // kv_heads
    depth = w_query.shape[0]
    half = w_query.shape[1] // 2
    new = new_query.shape[1]
    count = new * HQ
    bf16, f32 = jnp.bfloat16, jnp.float32

    head_mask = (jnp.arange(HQ)[:, None] // group) == (jnp.arange(kv_width)[None, :] // HD)
    head_wide = jnp.where(head_mask, jnp.tile(reward_head.reshape(HQ, HD), (1, kv_heads)), 0.0)
    head_two = jnp.concatenate(
        (*split_two(head_wide), jnp.zeros((HD - 2 * HQ, kv_width), bf16)), axis=0
    )
    last = step_hidden.reshape(beams, step_len, width)[:, step_len - 1]
    rows = last.reshape(beams, n // 2, 2 * depth).transpose(1, 0, 2)

    smem = pl.BlockSpec(memory_space=pltpu.SMEM)
    vmem = pl.BlockSpec(memory_space=pltpu.VMEM)
    hbm = pl.BlockSpec(memory_space=pl.ANY)
    dma = pltpu.SemaphoreType.DMA
    decoded, rewards = pl.pallas_call(
        functools.partial(score_kernel, n),
        out_shape=(
            jax.ShapeDtypeStruct((beams, count, HD), bf16),
            jax.ShapeDtypeStruct((beams, HD), f32),
        ),
        in_specs=[smem] * 4 + [vmem] * 6 + [hbm] * 3,
        out_specs=(vmem, vmem),
        scratch_shapes=[
            pltpu.VMEM(step_hidden.shape, bf16),
            pltpu.VMEM(prm_cache.shape, bf16),
            pltpu.VMEM(policy_pool.shape, bf16),
            pltpu.VMEM((n, depth, kv_width + HD), bf16),
            pltpu.VMEM((row_count, kv_width + HD), f32),
            pltpu.VMEM((beams, HQ, cache_len), f32),
            pltpu.VMEM((beams, HQ, cache_len), f32),
            pltpu.VMEM((beams, HQ, kv_width), bf16),
            pltpu.VMEM((beams, HQ, HD), f32),
            pltpu.VMEM((8, HD), f32),
            pltpu.VMEM((n, 8, HD), f32),
            pltpu.VMEM((n, count, HD), bf16),
            pltpu.VMEM((n, count, HD), bf16),
            pltpu.VMEM((n, beams, 2 * depth), bf16),
            pltpu.VMEM((2, depth, half), bf16),
            pltpu.VMEM((n, beams, half), bf16),
            pltpu.VMEM((n, beams, half), bf16),
            pltpu.VMEM((n, count, HD), bf16),
            pltpu.VMEM((n, count, HD), bf16),
            pltpu.VMEM((n, 8, HD), f32),
            pltpu.VMEM((n, 8, HD), f32),
            dma((6, n)),
            dma((6, n)),
            dma((2,)),
            dma((2, n // 4)),
            dma((2, n // 4)),
            dma((2, 2, n // 4)),
            dma((3,)),
        ],
        compiler_params=pltpu.CompilerParams(
            collective_id=0, has_side_effects=True, vmem_limit_bytes=52 * 2**20
        ),
        cost_estimate=pl.CostEstimate(
            flops=4 * 10**9, bytes_accessed=20 * 2**20, transcendentals=0
        ),
    )(
        lengths,
        page_table,
        placement,
        parents,
        rows,
        w_query,
        w_keyval,
        head_two,
        new_query.reshape(beams, count, HD),
        new_keyval.reshape(beams, new * 2 * kv_heads, HD),
        step_hidden,
        prm_cache,
        policy_pool,
    )
    return (rewards[:, 0], decoded.reshape(beams, new, HQ * HD))


def solution(mesh):
    in_specs = (
        P(("groups", "fsdp"), None),
        P(("groups", "fsdp"), None, None),
        P(("groups", "fsdp")),
        P("fsdp", None),
        P("fsdp", None),
        P(),
        P("groups"),
        P("groups"),
        P(("groups", "fsdp"), None),
        P(("groups", "fsdp"), None, None),
        P(("groups", "fsdp"), None, None),
        P(("groups", "fsdp"), None, None),
    )
    out_specs = (P(("groups", "fsdp")), P(("groups", "fsdp"), None, None))
    return jax.shard_map(shards, mesh=mesh, in_specs=in_specs, out_specs=out_specs, check_vma=False)
```

time: 110 us -> 94 us (0.85)
  Pallas kernels: 58.8 us -> 82.8 us
  waiting for transfers between devices: 14.4 us -> 0 us
  between operations: 14.2 us -> 0.69 us
  local copies, waits for them, and re-layouts: 18.6 us -> 9.83 us
  other arithmetic: 1.93 us -> 0.24 us
  matrix products: 1.12 us -> 0 us
    pallas_call x2 -> x1, Pallas kernels: 58.8 us -> 82.8 us  [shards(): pl.pallas_call(functools.partial(score_kernel, n), out_shape=(jax.ShapeDt...]
    all_gather x1 -> x0, waiting for transfers between devices: 14.4 us -> none  [shards(): weights = lax.all_gather(own_weights, 'fsdp', axis=0, tiled=True)]
    unnamed x16 -> x9, local copies, waits for them, and re-layouts: 10.5 us -> 3.8 us
    dot_general x1 -> x0, matrix products: 1.12 us -> none  [dot_last(): lax.dot_general(a, b, (((1,), (1,)), ((), ())), preferred_element_type=jn...]
  transfers between devices with their start and end apart: 1 -> 0, of which waited for: 1 -> 0; matrix products, arithmetic and copies ran while one was open for 7% -> 0% of each run, Pallas kernels for 43% -> 0%
where the time goes in v1:
time: 94 us; the launch traced here: 93.6 us
  Pallas kernels  82.8 us (88%)
  local copies, waits for them, and re-layouts  9.83 us (10%)
    pallas_call x1, Pallas kernels, shards(): pl.pallas_call(functools.partial(score_kernel, n), out_shape=(jax.ShapeDt...  82.8 us
    unnamed x9, local copies, waits for them, and re-layouts  3.8 us
    slice x1, local copies, waits for them, and re-layouts, shards(): last = step_hidden.reshape(beams, step_len, width)[:, step_len - 1]  2.03 us

profile of v1, /device:TPU:0, one launch (start us, length us, event | category | flops | bytes accessed | tf_op | source)
XLA Modules:
  0.0 93.6 jit_solution(16525739597253706440)
XLA Ops:
  0.7 0.1 pad.2.clone
  0.7 0.8 copy.17.pages
  1.5 0.7 tile.11
  2.2 0.1 subtract_convert_fusion
  2.3 0.1 fusion
  2.3 0.9 reshape.96.keyval_ref
  3.2 0.1 maximum_maximum_fusion.head_ref
  3.3 1.0 %reshape.95.query_ref = bf16[16,32,128]{2,1,0:T(8,128)(2,1)S(1)} reshape(bf16[16,2,2048]{2,1,0:T(2,128)(2,1)} %param.22) | data formatting | bytes 262144 | tf_op jit(solution)/shard_map/reshape | solution.py:535
  4.3 2.0 %slice_reduce_fusion = bf16[16,4096]{1,0:T(8,128)(2,1)S(1)} fusion(bf16[16,32,4096]{2,1,0:T(8,128)(2,1)} %bitcast.22), kind=kLoop, calls=%fused_computation | loop fusion | bytes 262144 | tf_op jit(solution)/shard_map/slice | solution.py:475
  6.4 0.0 copy-start
  6.4 1.0 %copy-done = bf16[256,1024]{1,0:T(8,128)(2,1)S(1)} copy-done((bf16[256,1024]{1,0:T(8,128)(2,1)S(1)}, bf16[256,1024]{1,0:T(8,128)(2,1)}, u32[]{:S(2)}) %copy-start) | copy-done | bytes 524312
  7.4 0.0 copy-start.1
  7.4 0.7 copy-done.1
  8.1 0.0 copy-start.2
  8.1 0.7 copy-done.2
  8.8 0.0 copy-start.3
  8.8 0.7 copy-done.3
  9.4 82.8 %shard_map.131 = (bf16[16,32,128]{2,1,0:T(8,128)(2,1)S(1)}, f32[16,128]{1,0:T(8,128)S(1)}) custom-call(s32[16]{0:T(128)S(1)} %copy-done.3, s32[16,2]{1,0:T(8,128)S(1)} %copy.17.pages, s32[256]{0:T(256)S(1)} %copy-done.1, s32[256]{0:T(256)S(1)} %copy-done.2, bf16[8,16,512]{2,1,0:T(8,128)(2,1)S(1)} %bitcast.18, bf16[256,2048]{1,0:T(8,128)(2,1)} %wq_ref.1, ...), custom_call_target="tpu_custom_call" | custom-call | flops 4000000000 | bytes 20971520 | tf_op jit(solution)/shard_map/pallas_call | solution.py:482
  92.3 0.6 slice_reduce_fusion.1
  92.9 0.7 reshape.97
  (4 shorter events, 0.0 us)
Async XLA Ops:
  6.4 1.0 %copy-start = (bf16[256,1024]{1,0:T(8,128)(2,1)S(1)}, bf16[256,1024]{1,0:T(8,128)(2,1)}, u32[]{:S(2)}) copy-start(bf16[256,1024]{1,0:T(8,128)(2,1)} %wkv_ref.1) | copy-start | bytes 1572868
  7.4 0.7 copy-start.1
  8.1 0.7 copy-start.2
  8.8 0.7 copy-start.3
